TPU v7x, 768 devices: a whole 4x8x12 slice. The times are simulated.
768 devices in a mesh: row: 64 (over y, x, core), col: 12 (over z).
Axes of the slice: x: 4, y: 8, z: 12, core: 2. Of those that a mesh axis runs over, the one named last changes fastest.
Arguments:
- matrix: float32 [9216, 9216], P('row', 'col'), as said below
Outputs:
- factored: float32 [9216, 9216], P('row', 'col')
Inputs may be any that keep to these rules, and one draw needn't show every extreme that they name: `matrix`: Off-diagonal entries are of order one; each diagonal entry lies between 4 * sqrt(256) and 8 * sqrt(256) times that.
All inputs are finite; a program needn't handle non-finite values.
Results may differ from a plain program's by a relative error of at most 0.0001.
Values sent between devices are 32-bit elements; how exact they have to be, the bound alone decides.
A program may use at most 32 MiB of HBM per device.

v0:
```python
import jax
import jax.numpy as jnp
from jax import lax
from jax.sharding import PartitionSpec as P

B = 256
STEPS = 2


def from_root(array, axis, root):
    mine = lax.axis_index(axis) == root
    return lax.psum(jnp.where(mine, array, jnp.zeros_like(array)), axis)


def mult(left, right):
    return jnp.dot(left, right, precision=lax.Precision.HIGHEST, preferred_element_type=jnp.float32)


def spans(lead, width, extent):
    result = []
    for owner in range(lead // extent, (lead + width - 1) // extent + 1):
        low = max(lead, owner * extent) - owner * extent
        high = min(lead + width, (owner + 1) * extent) - owner * extent
        result.append((owner, low, high))
    return result


def rows_plain(tile, lead, rows):
    pieces = [from_root(tile[low:high], "row", owner) for owner, low, high in spans(lead, B, rows)]
    return jnp.concatenate(pieces, axis=0)


def cols_joined(stacked, lead, cols):
    pieces = [
        from_root(stacked[:, low:high], "col", owner) for owner, low, high in spans(lead, B, cols)
    ]
    return pieces[0]


def inverse_of(block, eye):
    inverse = 1.0 / jnp.diagonal(block)
    first = inverse[:, None] * (2.0 * eye - block * inverse[None, :])
    return mult(first, 2.0 * eye - mult(block, first))


def on_device(matrix):
    rows, cols = matrix.shape
    row_ids = lax.axis_index("row") * rows + jnp.arange(rows, dtype=jnp.int32)[:, None]
    col_ids = lax.axis_index("col") * cols + jnp.arange(cols, dtype=jnp.int32)[None, :]
    eye = jnp.eye(B, dtype=jnp.float32)
    tile = matrix
    for step in range(STEPS):
        lead = step * B
        upper = rows_plain(tile, lead, rows)
        joined = cols_joined(jnp.concatenate([tile, upper], axis=0), lead, cols)
        lower = mult(joined[:rows], inverse_of(joined[rows:], eye))
        update = mult(lower, upper)
        picked = jnp.take(lower, jnp.clip(col_ids[0] - lead, 0, B - 1), axis=1)
        below = row_ids >= lead + B
        right = col_ids >= lead + B
        inside = (col_ids >= lead) & (col_ids < lead + B)
        tile = jnp.where(below & right, tile - update, jnp.where(below & inside, picked, tile))
    return tile


def solution(mesh):
    return jax.shard_map(
        on_device,
        mesh=mesh,
        in_specs=(P("row", "col"),),
        out_specs=P("row", "col"),
        check_vma=False,
    )
```

profile of v0, /device:TPU:6, one launch (start us, length us, event | category | flops | bytes accessed | tf_op | source)
XLA Modules:
  0.0 682.0 jit_solution(6993202399878267698)
XLA Ops:
  6.5 0.0 all-reduce.13.cloned.1.call-start
  6.5 1.8 slice_select_fusion
  8.3 0.0 copy-done.2
  8.3 0.8 broadcast_select_fusion.1
  9.1 0.0 all-reduce.13.cloned.1.call-update
  9.1 0.0 all-reduce.7.cloned.1.call-start
  9.2 212.7 %all-reduce.13.cloned.1.call-done = (f32[112,768]{1,0:T(8,128)}, f32[144,768]{1,0:T(8,128)}) async-done(((f32[112,768]{1,0:T(8,128)}, f32[144,768]{1,0:T(8,128)}), (f32[112,768]{1,0:T(8,128)}, f32[144,768]{1,0:T(8,128)})) %all-reduce.13.cloned.1.call-update) | async-done | bytes 786448 | tf_op jit(solution)/shard_map/psum | solution.py:12
  221.9 1.7 fusion.11
  223.7 0.0 all-reduce.7.cloned.1.call-update
  223.7 0.0 all-reduce.11.cloned.1.call-start
  223.8 114.1 %all-reduce.7.cloned.1.call-done = f32[400,256]{1,0:T(8,128)} async-done(((f32[400,256]{1,0:T(8,128)}), f32[400,256]{1,0:T(8,128)}) %all-reduce.7.cloned.1.call-update) | async-done | bytes 409616 | tf_op jit(solution)/shard_map/psum | solution.py:12
  338.0 0.9 slice-done.1
  338.9 2.3 gather_fusion
  341.3 0.0 copy-done.1
  341.3 0.5 convolution_subtract_fusion.3
  341.7 0.4 fusion.17
  342.2 0.3 fusion.22
  342.5 0.1 copy.6
  342.6 2.1 gather_fusion.2
  344.7 0.0 copy-start.3
  344.7 0.0 copy-start.5
  344.7 0.2 copy.7
  345.0 0.8 copy-done.3
  345.7 0.1 copy-done.5
  345.8 1.5 broadcast_select_fusion
  347.3 0.6 slice_select_fusion.2
  347.9 0.7 slice_select_fusion.1
  348.6 0.0 all-reduce.11.cloned.1.call-update
  348.7 0.0 all-reduce.9.cloned.1.call-start
  348.7 201.7 %all-reduce.11.cloned.1.call-done = (f32[80,768]{1,0:T(8,128)}, f32[144,768]{1,0:T(8,128)}, f32[32,768]{1,0:T(8,128)}) async-done(((f32[80,768]{1,0:T(8,128)}, f32[144,768]{1,0:T(8,128)}, f32[32,768]{1,0:T(8,128)}), (f32[80,768]{1,0:T(8,128)}, f32[144,768]{1,0:T(8,128)}, f32[32,768]{1,0:T(8,128)})) %all-reduce.11.cloned.1.call-update) | async-done | bytes 786448 | tf_op jit(solution)/shard_map/psum | solution.py:12
  550.5 1.7 fusion.10
  552.2 0.0 all-reduce.9.cloned.1.call-update
  552.3 113.8 %all-reduce.9.cloned.1.call-done = f32[400,256]{1,0:T(8,128)} async-done(((f32[400,256]{1,0:T(8,128)}), f32[400,256]{1,0:T(8,128)}) %all-reduce.9.cloned.1.call-update) | async-done | bytes 409616 | tf_op jit(solution)/shard_map/psum | solution.py:12
  666.1 0.9 slice-done
  667.1 2.3 gather_fusion.1
  669.4 0.0 copy-done
  669.4 0.5 convolution_subtract_fusion.2
  669.9 0.4 fusion.14
  670.3 0.3 fusion.20
  670.6 0.1 copy.8
  670.8 2.1 gather_fusion.3
  672.9 0.0 copy-start.4
  672.9 0.0 copy-start.6
  672.9 0.2 copy.9
  673.1 0.8 copy-done.4
  673.9 0.1 copy-done.6
  674.0 0.1 copy-done.7
  674.0 1.4 fusion
  (19 shorter events, 0.1 us)
Async XLA Ops:
  6.5 1.8 copy-start.2
  6.5 215.4 %all-reduce.13.cloned.1.call-start = ((), (), s32[]{:S(2)}) async-start(), calls=%async_computation.3 | async-start | bytes 1572864 | tf_op jit(solution)/shard_map/psum | solution.py:12
  9.1 328.8 %all-reduce.7.cloned.1.call-start = ((), (), s32[]{:S(2)}) async-start(), calls=%async_computation | async-start | bytes 819200 | tf_op jit(solution)/shard_map/psum | solution.py:12
  223.7 326.7 %all-reduce.11.cloned.1.call-start = ((), (), s32[]{:S(2)}) async-start(), calls=%async_computation.2 | async-start | bytes 1572864 | tf_op jit(solution)/shard_map/psum | solution.py:12
  337.9 0.9 slice-start.1
  338.9 2.4 copy-start.1
  344.7 1.0 copy-start.3
  344.7 1.1 copy-start.5
  348.7 317.4 %all-reduce.9.cloned.1.call-start = ((), (), s32[]{:S(2)}) async-start(), calls=%async_computation.1 | async-start | bytes 819200 | tf_op jit(solution)/shard_map/psum | solution.py:12
  666.1 0.9 slice-start
  667.1 2.4 copy-start
  672.9 1.0 copy-start.4
  672.9 1.1 copy-start.6
  672.9 1.1 copy-start.7
Sparse Core Ops, SparseCore 0:
  10.9 211.0 all-reduce.12
  224.4 113.4 all-reduce.6
  348.8 201.6 all-reduce.10
  552.8 113.2 all-reduce.8
where the time goes:
time: 682 us
  waiting for transfers between devices  642 us (94%)
  between operations  13.4 us (2%)
  local copies, waits for them, and re-layouts  13.3 us (2%)
  other arithmetic  7.52 us (1%)
    psum x4, waiting for transfers between devices, from_root(): return lax.psum(jnp.where(mine, array, jnp.zeros_like(array)), axis)  642 us
  transfers between devices with their start and end apart: 4, of which 4 were waited for; matrix products, arithmetic and copies ran while one was open for 0% of the time, Pallas kernels for 0%

commit v1 on v0

v1 whole, which is shorter than its diff:
```python
import jax
import jax.numpy as jnp
from jax import lax
from jax.experimental import pallas as pl
from jax.experimental.pallas import tpu as pltpu
from jax.sharding import PartitionSpec as P

B = 256
ROWS, COLS = 144, 768
NX, NY, NZ = 4, 8, 12
CH = 16
NCH = ROWS // CH
LAST = (2 * B - 3 * ROWS) // CH
LAG = 4
PARTS = ((0, 2 * B), (2 * B, COLS - 2 * B))
MESH = pl.DeviceIdType.MESH
F1, F2, FAR, EX, SIBP, SIBS = range(6)
RP, RX, RSP, RSS = range(4)

Y_TREE = {0: (2, 6), 2: (3, 1), 6: (5, 7), 3: (4, None)}
Z_TREE = {0: (3, 9), 3: (5, 2), 5: (6, 4), 2: (1, None), 9: (8, 10), 8: (7, None), 10: (11, None)}


def lookup(value, table):
    found = jnp.int32(0)
    entry = jnp.int32(0)
    for key, item in table.items():
        found = jnp.where(value == key, 1, found)
        entry = jnp.where(value == key, item, entry)
    return found, entry


def branch(tree, which):
    return {k: v[which] for k, v in tree.items() if v[which] is not None}


def parents(tree):
    return {child: k for k, v in tree.items() for child in v if child is not None}


def split(v):
    high = v.astype(jnp.bfloat16)
    low = (v - high.astype(jnp.float32)).astype(jnp.bfloat16)
    return high, low


def dot(a, b):
    return jnp.dot(a, b, preferred_element_type=jnp.float32)


def mult(a, b):
    ah, al = split(a)
    bh, bl = split(b)
    return dot(ah, bh) + (dot(ah, bl) + dot(al, bh))


def inverse_of(block):
    i = lax.broadcasted_iota(jnp.int32, (B, B), 0)
    j = lax.broadcasted_iota(jnp.int32, (B, B), 1)
    diag = jnp.where(i == j, block, 0.0)
    two = jnp.where(i == j, 2.0, 0.0)
    across = 1.0 / jnp.sum(diag, axis=0, keepdims=True)
    down = 1.0 / jnp.sum(diag, axis=1, keepdims=True)
    first = down * (two - block * across)
    return mult(first, two - mult(block, first))


def kernel(m_ref, o_ref, tile, ubuf, wbuf, low0, ssem, rsem, zssem, zrsem, lsem, osem):
    r = lax.axis_index("row")
    z = lax.axis_index("col")
    y, x, c = r // (2 * NX), (r // 2) % NX, r % 2
    odd = x % 2
    other = x + 1 - 2 * odd

    def at(yy, xx, cc, zz):
        return ((yy * NX + xx) * 2 + cc, zz)

    has_f1, y1 = lookup(y, branch(Y_TREE, 0))
    has_f2, y2 = lookup(y, branch(Y_TREE, 1))
    has_up, yup = lookup(y, parents(Y_TREE))
    source = jnp.where((y == 0) & (x < 2), 1, 0)
    far_in = jnp.where((y == 0) & (x >= 2), 1, 0)
    has_z1, z1 = lookup(z, branch(Z_TREE, 0))
    has_z2, z2 = lookup(z, branch(Z_TREE, 1))
    has_zup, zup = lookup(z, parents(Z_TREE))
    xfar = (x + 2) % NX

    mine = c + 2 * odd
    theirs = c + 2 - 2 * odd
    n_mine = jnp.where(mine == 3, LAST, NCH)
    n_theirs = jnp.where(theirs == 3, LAST, NCH)
    sib_p = 1 - c + 2 * odd
    sib_s = 1 - c + 2 - 2 * odd
    n_sib_p = jnp.where(sib_p == 3, LAST, NCH)
    n_sib_s = jnp.where(sib_s == 3, LAST, NCH)

    load = pltpu.make_async_copy(m_ref, tile, lsem.at[0])
    load.start()
    full = (source == 1) & (mine != 3)
    part = (source == 1) & (mine == 3)

    def own(n):
        return pltpu.make_async_copy(
            m_ref.at[pl.ds(0, n)], ubuf.at[pl.ds(pl.multiple_of(mine * ROWS, CH), n)], lsem.at[1]
        )

    @pl.when(full)
    def _():
        own(ROWS).start()

    @pl.when(part)
    def _():
        own(LAST * CH).start()

    bar = pltpu.get_barrier_semaphore()

    def hello(where):
        pl.semaphore_signal(bar, inc=1, device_id=where, device_id_type=MESH)

    @pl.when(has_up == 1)
    def _():
        hello(at(yup, x, c, z))

    @pl.when(far_in == 1)
    def _():
        hello(at(0, xfar, c, z))

    @pl.when(has_zup == 1)
    def _():
        hello((r, zup))

    hello(at(y, other, c, z))
    hello(at(y, x, 1 - c, z))
    pl.semaphore_wait(bar, 2 + has_f1 + has_f2 + source + has_z1 + has_z2)

    @pl.when(full)
    def _():
        own(ROWS).wait()

    @pl.when(part)
    def _():
        own(LAST * CH).wait()

    def rows_of(block, i):
        return pl.ds(pl.multiple_of(block * ROWS + i * CH, CH), CH)

    def copy(p, block, i, kind, got, where):
        start, width = PARTS[p]
        ref = ubuf.at[rows_of(block, i), pl.ds(start, width)]
        return pltpu.make_async_remote_copy(
            src_ref=ref,
            dst_ref=ref,
            send_sem=ssem.at[p, kind, i],
            recv_sem=rsem.at[p, got, i],
            device_id=where,
            device_id_type=MESH,
        )

    sends = (
        (F1, has_f1, RP, at(y1, x, c, z)),
        (F2, has_f2, RP, at(y2, x, c, z)),
        (FAR, source, RP, at(0, xfar, c, z)),
        (EX, None, RX, at(y, other, c, z)),
        (SIBP, None, RSP, at(y, x, 1 - c, z)),
    )
    sibling = at(y, x, 1 - c, z)

    def plane(p):
        def body(i, carry):
            @pl.when(i < n_mine)
            def _():
                @pl.when(source == 0)
                def _():
                    copy(p, mine, i, F1, RP, sibling).wait_recv()

                for kind, has, got, where in sends:
                    if has is None:
                        copy(p, mine, i, kind, got, where).start()
                    else:

                        @pl.when(has == 1)
                        def _(kind=kind, got=got, where=where):
                            copy(p, mine, i, kind, got, where).start()

            j = i - LAG

            @pl.when((j >= 0) & (j < n_theirs))
            def _():
                copy(p, theirs, j, EX, RX, sibling).wait_recv()
                copy(p, theirs, j, SIBS, RSS, sibling).start()

            return carry

        lax.fori_loop(0, NCH + LAG, body, 0)

        def got(i, carry):
            @pl.when(i < n_sib_p)
            def _():
                copy(p, sib_p, i, SIBP, RSP, sibling).wait_recv()

            @pl.when(i < n_sib_s)
            def _():
                copy(p, sib_s, i, SIBS, RSS, sibling).wait_recv()

            return carry

        lax.fori_loop(0, NCH, got, 0)

    def sent(p):
        def body(i, carry):
            @pl.when(i < n_mine)
            def _():
                for kind, has, got, where in sends:
                    if has is None:
                        copy(p, mine, i, kind, got, where).wait_send()
                    else:

                        @pl.when(has == 1)
                        def _(kind=kind, got=got, where=where):
                            copy(p, mine, i, kind, got, where).wait_send()

            @pl.when(i < n_theirs)
            def _():
                copy(p, theirs, i, SIBS, RSS, sibling).wait_send()

            return carry

        lax.fori_loop(0, NCH, body, 0)

    def wcopy(i, kind, where):
        ref = wbuf.at[pl.ds(pl.multiple_of(i * CH, CH), CH)]
        return pltpu.make_async_remote_copy(
            src_ref=ref,
            dst_ref=ref,
            send_sem=zssem.at[kind, i],
            recv_sem=zrsem.at[i],
            device_id=where,
            device_id_type=MESH,
        )

    down = ((0, has_z1, (r, z1)), (1, has_z2, (r, z2)))

    def along(i, carry):
        @pl.when(has_zup == 1)
        def _():
            wcopy(i, 0, (r, z1)).wait_recv()

        for kind, has, where in down:

            @pl.when(has == 1)
            def _(kind=kind, where=where):
                wcopy(i, kind, where).start()

        return carry

    def along_sent(i, carry):
        for kind, has, where in down:

            @pl.when(has == 1)
            def _(kind=kind, where=where):
                wcopy(i, kind, where).wait_send()

        return carry

    row_id = r * ROWS + lax.broadcasted_iota(jnp.int32, (ROWS, B), 0)
    below0 = row_id >= B
    below1 = row_id >= 2 * B

    plane(0)
    load.wait()

    @pl.when(z == 0)
    def _():
        second0 = inverse_of(ubuf[:B, :B])
        s0 = split(second0)

        def times(a, pair):
            ah, al = split(a)
            return dot(ah, pair[0]) + (dot(ah, pair[1]) + dot(al, pair[0]))

        l10 = times(ubuf[B : 2 * B, :B], s0)
        lower0 = times(tile[:, :B], s0)
        u01 = split(ubuf[:B, B : 2 * B])
        block1 = ubuf[B : 2 * B, B : 2 * B] - times(l10, u01)
        panel1 = tile[:, B : 2 * B] - times(lower0, u01)
        lower1 = mult(panel1, inverse_of(block1))
        w0 = lower0 - mult(lower1, l10)
        wbuf[:, :B] = jnp.where(below1, w0, jnp.where(below0, lower0, 0.0))
        wbuf[:, B:] = jnp.where(below1, lower1, 0.0)
        low0[...] = lower0
        tile[:, B : 2 * B] = jnp.where(below1, lower1, jnp.where(below0, panel1, tile[:, B : 2 * B]))
        lax.fori_loop(0, NCH, along, 0)

    plane(1)

    @pl.when(z != 0)
    def _():
        lax.fori_loop(0, NCH, along, 0)

    wh, wl = split(wbuf[...])

    def update(start):
        uh, ul = split(ubuf[:, start : start + B])
        tile[:, start : start + B] -= dot(wh, uh) + (dot(wh, ul) + dot(wl, uh))

    @pl.when(z != 0)
    def _():
        update(0)
        update(B)

    update(2 * B)

    @pl.when(z == 0)
    def _():
        tile[:, :B] = jnp.where(below0, low0[...], tile[:, :B])

    out = pltpu.make_async_copy(tile, o_ref, osem)
    out.start()
    sent(0)
    sent(1)
    lax.fori_loop(0, NCH, along_sent, 0)
    out.wait()


def on_device(matrix):
    return pl.pallas_call(
        kernel,
        out_shape=jax.ShapeDtypeStruct((ROWS, COLS), jnp.float32),
        in_specs=[pl.BlockSpec(memory_space=pl.ANY)],
        out_specs=pl.BlockSpec(memory_space=pl.ANY),
        scratch_shapes=[
            pltpu.VMEM((ROWS, COLS), jnp.float32),
            pltpu.VMEM((2 * B, COLS), jnp.float32),
            pltpu.VMEM((ROWS, 2 * B), jnp.float32),
            pltpu.VMEM((ROWS, B), jnp.float32),
            pltpu.SemaphoreType.DMA((2, 6, NCH)),
            pltpu.SemaphoreType.DMA((2, 4, NCH)),
            pltpu.SemaphoreType.DMA((2, NCH)),
            pltpu.SemaphoreType.DMA((NCH,)),
            pltpu.SemaphoreType.DMA((2,)),
            pltpu.SemaphoreType.DMA,
        ],
        compiler_params=pltpu.CompilerParams(
            collective_id=0, has_side_effects=True, vmem_limit_bytes=40 << 20
        ),
        name="panel_steps",
    )(matrix)


def solution(mesh):
    return jax.shard_map(
        on_device,
        mesh=mesh,
        in_specs=(P("row", "col"),),
        out_specs=P("row", "col"),
        check_vma=False,
    )
```

time: 682 us -> 59 us (0.09)
  the two profiles are of different devices: /device:TPU:6 before, /device:TPU:102 now
where the time goes in v1:
time: 59 us; the launch traced here: 58.8 us
  Pallas kernels  57 us (97%)
  local copies, waits for them, and re-layouts  1.78 us (3%)
    pallas_call x1, Pallas kernels, on_device(): pl.pallas_call(kernel, out_shape=jax.ShapeDtypeStruct((ROWS, COLS), jnp.f...  57 us
    unnamed x3, local copies, waits for them, and re-layouts  1.78 us

profile of v1, /device:TPU:102, one launch (start us, length us, event | category | flops | bytes accessed | tf_op | source)
XLA Modules:
  0.0 58.8 jit_solution(15663308193484778422)
XLA Ops:
  0.0 0.0 copy-start
  0.0 1.0 %copy-done = f32[144,768]{1,0:T(8,128)S(1)} copy-done((f32[144,768]{1,0:T(8,128)S(1)}, f32[144,768]{1,0:T(8,128)}, u32[]{:S(2)}) %copy-start) | copy-done | bytes 442392
  1.0 57.0 %panel_steps.1 = f32[144,768]{1,0:T(8,128)S(1)} custom-call(f32[144,768]{1,0:T(8,128)S(1)} %copy-done), custom_call_target="tpu_custom_call" | custom-call | tf_op jit(solution)/shard_map/panel_steps/pallas_call | solution.py:326
  58.0 0.8 %copy.3 = f32[144,768]{1,0:T(8,128)} copy(f32[144,768]{1,0:T(8,128)S(1)} %panel_steps.1) | data formatting | bytes 884736
Async XLA Ops:
  0.0 1.0 %copy-start = (f32[144,768]{1,0:T(8,128)S(1)}, f32[144,768]{1,0:T(8,128)}, u32[]{:S(2)}) copy-start(f32[144,768]{1,0:T(8,128)} %m_ref.1) | copy-start | bytes 1327108

commit v2 on v1

v2 whole, which is shorter than its diff:
```python
import jax
import jax.numpy as jnp
from jax import lax
from jax.experimental import pallas as pl
from jax.experimental.pallas import tpu as pltpu
from jax.sharding import PartitionSpec as P

B = 256
ROWS, COLS = 144, 768
NX, NY, NZ = 4, 8, 12
CH = 16
NCH = ROWS // CH
CZ = 8
NCZ = ROWS // CZ
LAST = (2 * B - 3 * ROWS) // CH
PARTS = ((0, 2 * B), (2 * B, COLS - 2 * B))
MESH = pl.DeviceIdType.MESH
VMEM = 54500 << 10
F1, F2, FAR, EX, SIBP, SIBS, FAR2, G1, G2 = range(9)
RP, RX, RSP, RSS = range(4)

Y_TREE = {0: (2, 6), 2: (3, 1), 6: (5, 7), 3: (4, None)}
Z_TREE = {
    0: (1, 9),
    1: (2, None),
    2: (3, None),
    3: (4, None),
    9: (6, 10),
    10: (11, None),
    6: (5, 7),
    7: (8, None),
}
EARLY = (5, 6)
PASS_FIRST = 9


def lookup(value, table):
    found = jnp.int32(0)
    entry = jnp.int32(0)
    for key, item in table.items():
        found = jnp.where(value == key, 1, found)
        entry = jnp.where(value == key, item, entry)
    return found, entry


def branch(tree, which):
    return {k: v[which] for k, v in tree.items() if v[which] is not None}


def parents(tree):
    return {child: k for k, v in tree.items() for child in v if child is not None}


def split(v):
    high = v.astype(jnp.bfloat16)
    low = (v - high.astype(jnp.float32)).astype(jnp.bfloat16)
    return high, low


def dot(a, b):
    return jnp.dot(a, b, preferred_element_type=jnp.float32)


def mult(a, b):
    ah, al = split(a)
    bh, bl = split(b)
    return dot(ah, bh) + (dot(ah, bl) + dot(al, bh))


def inverse_of(block):
    i = lax.broadcasted_iota(jnp.int32, (B, B), 0)
    j = lax.broadcasted_iota(jnp.int32, (B, B), 1)
    diag = jnp.where(i == j, block, 0.0)
    two = jnp.where(i == j, 2.0, 0.0)
    across = 1.0 / jnp.sum(diag, axis=0, keepdims=True)
    down = 1.0 / jnp.sum(diag, axis=1, keepdims=True)
    first = down * (two - block * across)
    return mult(first, two - mult(block, first))


def kernel(m_ref, o_ref, tile, ubuf, wbuf, low0, uhigh, ulow, ssem, rsem, zssem, zrsem, lsem, osem, zready):
    r = lax.axis_index("row")
    z = lax.axis_index("col")
    y, x, c = r // (2 * NX), (r // 2) % NX, r % 2
    odd = x % 2
    other = x + 1 - 2 * odd
    side = jnp.where((x == 1) | (x == 2), 1, 0)
    idle = jnp.where(r == 0, 1, 0)
    busy = 1 - idle

    def at(yy, xx, cc, zz):
        return ((yy * NX + xx) * 2 + cc, zz)

    has_f1, y1 = lookup(y, branch(Y_TREE, 0))
    has_f2, y2 = lookup(y, branch(Y_TREE, 1))
    has_up, yup = lookup(y, parents(Y_TREE))
    source = jnp.where((y == 0) & (x < 2), 1, 0)
    far_in = jnp.where((y == 0) & (x >= 2), 1, 0)
    has_z1, z1 = lookup(z, branch(Z_TREE, 0))
    has_z2, z2 = lookup(z, branch(Z_TREE, 1))
    has_zup, zup = lookup(z, parents(Z_TREE))
    has_z1, has_z2, has_zup = has_z1 * busy, has_z2 * busy, has_zup * busy
    early, _ = lookup(z, {k: 0 for k in EARLY})
    early1, _ = lookup(z1, {k: 0 for k in EARLY})
    early2, _ = lookup(z2, {k: 0 for k in EARLY})
    early1, early2 = has_z1 * early1, has_z2 * early2
    late1, late2 = has_z1 - early1, has_z2 - early2
    xfar = NX - 1 - x
    ex_to = (jnp.where(r == 2, 1, (y * NX + other) * 2 + c), z)
    ex_got = jnp.where(r == 2, RSS, RX)
    straight = jnp.where((z == 0) & (r == 0), 1, 0)
    third = jnp.where((z == 0) & (c == 0) & (x == 2), 1, 0)
    has_ex = jnp.where((z == 0) & (c == 0) & (x == 3), 0, 1)
    has_sib = jnp.where(r == 1, 0, 1)

    mine = c + 2 * side
    theirs = c + 2 - 2 * side
    n_mine = jnp.where(mine == 3, LAST, NCH)
    n_theirs = jnp.where(theirs == 3, LAST, NCH)
    sib_p = 1 - c + 2 * side
    sib_s = 1 - c + 2 - 2 * side
    n_sib_p = jnp.where(sib_p == 3, LAST, NCH)
    n_sib_s = jnp.where(sib_s == 3, LAST, NCH)

    load = pltpu.make_async_copy(m_ref, tile, lsem.at[0])
    load.start()
    full = (source == 1) & (mine != 3)
    part = (source == 1) & (mine == 3)

    def own(n):
        return pltpu.make_async_copy(
            m_ref.at[pl.ds(0, n)], ubuf.at[pl.ds(pl.multiple_of(mine * ROWS, CH), n)], lsem.at[1]
        )

    @pl.when(full)
    def _():
        own(ROWS).start()

    @pl.when(part)
    def _():
        own(LAST * CH).start()

    bar = pltpu.get_barrier_semaphore()

    def hello(where):
        pl.semaphore_signal(bar, inc=1, device_id=where, device_id_type=MESH)

    @pl.when(has_up == 1)
    def _():
        hello(at(yup, x, c, z))

    @pl.when(far_in == 1)
    def _():
        hello(at(0, xfar, c, z))

    @pl.when((has_zup == 1) & (early == 1))
    def _():
        hello((r, zup))

    @pl.when(late1 == 1)
    def _():
        hello((r, z1))

    @pl.when(late2 == 1)
    def _():
        hello((r, z2))

    @pl.when(busy == 1)
    def _():
        hello(at(y, x, 1 - c, z))

    @pl.when((busy == 1) & (third == 0))
    def _():
        hello(at(y, other, c, z))

    @pl.when((third == 1) & (r == 4))
    def _():
        hello((0, z))

    @pl.when(r == 1)
    def _():
        hello((2, z))

    greeted = jnp.where((has_zup == 1) & (early == 0), 1, 0)
    pl.semaphore_wait(bar, has_ex + has_sib + straight + has_f1 + has_f2 + source + early1 + early2 + greeted)

    @pl.when(greeted == 1)
    def _():
        pl.semaphore_signal(zready, inc=1, device_id=(r, zup), device_id_type=MESH)

    def rows_of(block, i):
        return pl.ds(pl.multiple_of(block * ROWS + i * CH, CH), CH)

    def copy(p, block, i, kind, got, where, own=False):
        start, width = PARTS[p]
        ref = ubuf.at[rows_of(block, i), pl.ds(start, width)]
        return pltpu.make_async_remote_copy(
            src_ref=m_ref.at[rows_of(0, i), pl.ds(start, width)] if own else ref,
            dst_ref=ref,
            send_sem=ssem.at[p, kind, i],
            recv_sem=rsem.at[p, got, i],
            device_id=where,
            device_id_type=MESH,
        )

    sibling = at(y, x, 1 - c, z)
    sends = (
        (FAR, source, RP, at(0, xfar, c, z)),
        (F1, has_f1, RP, at(y1, x, c, z)),
        (F2, has_f2, RP, at(y2, x, c, z)),
        (FAR2, straight, RX, (4, z)),
        (EX, has_ex, ex_got, ex_to),
        (SIBP, has_sib, RSP, sibling),
    )

    onward = (
        (G1, third * has_f1, RX, at(y1, x, c, z)),
        (G2, third * has_f2, RX, at(y2, x, c, z)),
        (SIBS, has_sib, RSS, sibling),
    )

    def first(p):
        def issue(i, own):
            for kind, has, got, where in sends:

                @pl.when(has == 1)
                def _(kind=kind, got=got, where=where):
                    copy(p, mine, i, kind, got, where, own).start()

        def body(i, carry):
            @pl.when(source == 1)
            def _():
                issue(i, True)

            @pl.when(source == 0)
            def _():
                copy(p, mine, i, F1, RP, sibling).wait_recv()
                issue(i, False)

            return carry

        lax.fori_loop(0, n_mine, body, 0)

    def second(p):
        def body(i, carry):
            copy(p, theirs, i, EX, RX, sibling).wait_recv()

            for kind, has, got, where in onward:

                @pl.when(has == 1)
                def _(kind=kind, got=got, where=where):
                    copy(p, theirs, i, kind, got, where).start()

            return carry

        def got_p(i, carry):
            copy(p, sib_p, i, SIBP, RSP, sibling).wait_recv()
            return carry

        def got_s(i, carry):
            copy(p, sib_s, i, SIBS, RSS, sibling).wait_recv()
            return carry

        @pl.when(busy == 1)
        def _():
            lax.fori_loop(0, n_theirs, body, 0)
            lax.fori_loop(0, n_sib_p, got_p, 0)
            lax.fori_loop(0, n_sib_s, got_s, 0)

    def sent(p):
        def body_p(i, carry):
            for kind, has, got, where in sends:

                @pl.when(has == 1)
                def _(kind=kind, got=got, where=where):
                    copy(p, mine, i, kind, got, where).wait_send()

            return carry

        def body_s(i, carry):
            for kind, has, got, where in onward:

                @pl.when(has == 1)
                def _(kind=kind, got=got, where=where):
                    copy(p, theirs, i, kind, got, where).wait_send()

            return carry

        lax.fori_loop(0, n_mine, body_p, 0)

        @pl.when(busy == 1)
        def _():
            lax.fori_loop(0, n_theirs, body_s, 0)

    def wcopy(i, kind, where):
        ref = wbuf.at[pl.ds(pl.multiple_of(i * CZ, CZ), CZ)]
        return pltpu.make_async_remote_copy(
            src_ref=ref,
            dst_ref=ref,
            send_sem=zssem.at[kind, i],
            recv_sem=zrsem.at[i],
            device_id=where,
            device_id_type=MESH,
        )

    down = ((0, has_z1, (r, z1)), (1, has_z2, (r, z2)))

    def along(i, carry):
        @pl.when(has_zup == 1)
        def _():
            wcopy(i, 0, (r, z1)).wait_recv()

        for kind, has, where in down:

            @pl.when(has == 1)
            def _(kind=kind, where=where):
                wcopy(i, kind, where).start()

        return carry

    def pass_on():
        @pl.when(late1 + late2 > 0)
        def _():
            pl.semaphore_wait(zready, late1 + late2)

        lax.fori_loop(0, NCZ, along, 0)

    def along_sent(i, carry):
        for kind, has, where in down:

            @pl.when(has == 1)
            def _(kind=kind, where=where):
                wcopy(i, kind, where).wait_send()

        return carry

    def give(k):
        cols = pl.ds(k * B, B)
        return pltpu.make_async_copy(tile.at[:, cols], o_ref.at[:, cols], osem.at[k])

    row_id = r * ROWS + lax.broadcasted_iota(jnp.int32, (ROWS, B), 0)
    below0 = row_id >= B
    below1 = row_id >= 2 * B

    ahead = (z != 0) | (source == 1)
    pass_first = (z == PASS_FIRST) & (busy == 1)
    first(0)

    @pl.when(ahead)
    def _():
        first(1)

    pl.when(pass_first)(pass_on)
    second(0)
    load.wait()

    @pl.when(full)
    def _():
        own(ROWS).wait()

    @pl.when(part)
    def _():
        own(LAST * CH).wait()

    @pl.when((z == 0) & (busy == 1))
    def _():
        second0 = inverse_of(ubuf[:B, :B])
        s0 = split(second0)

        def times(a, pair):
            ah, al = split(a)
            return dot(ah, pair[0]) + (dot(ah, pair[1]) + dot(al, pair[0]))

        l10 = times(ubuf[B : 2 * B, :B], s0)
        lower0 = times(tile[:, :B], s0)
        u01 = split(ubuf[:B, B : 2 * B])
        block1 = ubuf[B : 2 * B, B : 2 * B] - times(l10, u01)
        panel1 = tile[:, B : 2 * B] - times(lower0, u01)
        lower1 = mult(panel1, inverse_of(block1))
        w0 = lower0 - mult(lower1, l10)
        wbuf[:, :B] = jnp.where(below1, w0, jnp.where(below0, lower0, 0.0))
        wbuf[:, B:] = jnp.where(below1, lower1, 0.0)
        low0[...] = lower0
        tile[:, B : 2 * B] = jnp.where(below1, lower1, jnp.where(below0, panel1, tile[:, B : 2 * B]))
        pass_on()

    @pl.when(jnp.logical_not(ahead))
    def _():
        first(1)

    second(1)

    @pl.when((z != 0) & (busy == 1))
    def _():
        def prepare():
            for start in range(0, COLS, B):
                uhigh[:, start : start + B], ulow[:, start : start + B] = split(ubuf[:, start : start + B])

        pl.when(has_z1 == 0)(prepare)
        pl.when(jnp.logical_not(pass_first))(pass_on)
        pl.when(has_z1 == 1)(prepare)
        wh, wl = split(wbuf[...])
        for k in range(COLS // B):
            uh, ul = uhigh[:, k * B : (k + 1) * B], ulow[:, k * B : (k + 1) * B]
            tile[:, k * B : (k + 1) * B] -= dot(wh, uh) + (dot(wh, ul) + dot(wl, uh))
            give(k).start()

    @pl.when((z == 0) & (busy == 1))
    def _():
        tile[:, 2 * B :] -= mult(wbuf[...], ubuf[:, 2 * B :])
        tile[:, :B] = jnp.where(below0, low0[...], tile[:, :B])

    @pl.when((z == 0) | (idle == 1))
    def _():
        for k in range(COLS // B):
            give(k).start()

    sent(0)
    sent(1)
    lax.fori_loop(0, NCZ, along_sent, 0)
    for k in range(COLS // B):
        give(k).wait()


def on_device(matrix):
    return pl.pallas_call(
        kernel,
        out_shape=jax.ShapeDtypeStruct((ROWS, COLS), jnp.float32),
        in_specs=[pl.BlockSpec(memory_space=pltpu.HBM)],
        out_specs=pl.BlockSpec(memory_space=pl.ANY),
        scratch_shapes=[
            pltpu.VMEM((ROWS, COLS), jnp.float32),
            pltpu.VMEM((2 * B, COLS), jnp.float32),
            pltpu.VMEM((ROWS, 2 * B), jnp.float32),
            pltpu.VMEM((ROWS, B), jnp.float32),
            pltpu.VMEM((2 * B, COLS), jnp.bfloat16),
            pltpu.VMEM((2 * B, COLS), jnp.bfloat16),
            pltpu.SemaphoreType.DMA((2, 9, NCH)),
            pltpu.SemaphoreType.DMA((2, 4, NCH)),
            pltpu.SemaphoreType.DMA((2, NCZ)),
            pltpu.SemaphoreType.DMA((NCZ,)),
            pltpu.SemaphoreType.DMA((2,)),
            pltpu.SemaphoreType.DMA((COLS // B,)),
            pltpu.SemaphoreType.REGULAR,
        ],
        compiler_params=pltpu.CompilerParams(
            collective_id=0, has_side_effects=True, vmem_limit_bytes=VMEM
        ),
        name="panel_steps",
    )(matrix)


def solution(mesh):
    return jax.shard_map(
        on_device,
        mesh=mesh,
        in_specs=(P("row", "col"),),
        out_specs=P("row", "col"),
        check_vma=False,
    )
```

time: 59 us -> 44.8 us (0.76)
  the two profiles are of different devices: /device:TPU:102 before, /device:TPU:292 now
where the time goes in v2:
time: 44.8 us; the launch traced here: 44.7 us
  Pallas kernels  43.9 us (98%)
  local copies, waits for them, and re-layouts  0.76 us (2%)
    pallas_call x1, Pallas kernels, on_device(): pl.pallas_call(kernel, out_shape=jax.ShapeDtypeStruct((ROWS, COLS), jnp.f...  43.9 us

profile of v2, /device:TPU:292, one launch (start us, length us, event | category | flops | bytes accessed | tf_op | source)
XLA Modules:
  0.0 44.7 jit_solution(4009715996632554042)
XLA Ops:
  0.0 43.9 %panel_steps.1 = f32[144,768]{1,0:T(8,128)S(1)} custom-call(f32[144,768]{1,0:T(8,128)} %m_ref.1), custom_call_target="tpu_custom_call" | custom-call | tf_op jit(solution)/shard_map/panel_steps/pallas_call | solution.py:426
  43.9 0.8 %copy.3 = f32[144,768]{1,0:T(8,128)} copy(f32[144,768]{1,0:T(8,128)S(1)} %panel_steps.1) | data formatting | bytes 884736

commit v3 on v2

--- a/solution.py
+++ b/solution.py
@@ -17,7 +17,8 @@
 MESH = pl.DeviceIdType.MESH
 VMEM = 54500 << 10
 F1, F2, FAR, EX, SIBP, SIBS, FAR2, G1, G2 = range(9)
-RP, RX, RSP, RSS = range(4)
+RP, RX = range(2)
+SP, SS = range(2)
 
 Y_TREE = {0: (2, 6), 2: (3, 1), 6: (5, 7), 3: (4, None)}
 Z_TREE = {
@@ -78,7 +79,7 @@
     return mult(first, two - mult(block, first))
 
 
-def kernel(m_ref, o_ref, tile, ubuf, wbuf, low0, uhigh, ulow, ssem, rsem, zssem, zrsem, lsem, osem, zready):
+def kernel(m_ref, o_ref, tile, ubuf, wbuf, low0, uhigh, ulow, ssem, rsem, ysem, zssem, zrsem, lsem, osem, zready):
     r = lax.axis_index("row")
     z = lax.axis_index("col")
     y, x, c = r // (2 * NX), (r // 2) % NX, r % 2
@@ -106,8 +107,6 @@
     early1, early2 = has_z1 * early1, has_z2 * early2
     late1, late2 = has_z1 - early1, has_z2 - early2
     xfar = NX - 1 - x
-    ex_to = (jnp.where(r == 2, 1, (y * NX + other) * 2 + c), z)
-    ex_got = jnp.where(r == 2, RSS, RX)
     straight = jnp.where((z == 0) & (r == 0), 1, 0)
     third = jnp.where((z == 0) & (c == 0) & (x == 2), 1, 0)
     has_ex = jnp.where((z == 0) & (c == 0) & (x == 3), 0, 1)
@@ -119,8 +118,6 @@
     n_theirs = jnp.where(theirs == 3, LAST, NCH)
     sib_p = 1 - c + 2 * side
     sib_s = 1 - c + 2 - 2 * side
-    n_sib_p = jnp.where(sib_p == 3, LAST, NCH)
-    n_sib_s = jnp.where(sib_s == 3, LAST, NCH)
 
     load = pltpu.make_async_copy(m_ref, tile, lsem.at[0])
     load.start()
@@ -182,7 +179,7 @@
         hello((2, z))
 
     greeted = jnp.where((has_zup == 1) & (early == 0), 1, 0)
-    pl.semaphore_wait(bar, has_ex + has_sib + straight + has_f1 + has_f2 + source + early1 + early2 + greeted)
+    pl.semaphore_wait(bar, has_ex + straight + has_sib + has_f1 + has_f2 + source + early1 + early2 + greeted)
 
     @pl.when(greeted == 1)
     def _():
@@ -191,41 +188,59 @@
     def rows_of(block, i):
         return pl.ds(pl.multiple_of(block * ROWS + i * CH, CH), CH)
 
-    def copy(p, block, i, kind, got, where, own=False):
-        start, width = PARTS[p]
-        ref = ubuf.at[rows_of(block, i), pl.ds(start, width)]
+    def moved(p, rows, kind, recv, where, src=None):
+        ref = ubuf.at[rows, pl.ds(*PARTS[p])]
         return pltpu.make_async_remote_copy(
-            src_ref=m_ref.at[rows_of(0, i), pl.ds(start, width)] if own else ref,
+            src_ref=ref if src is None else src,
             dst_ref=ref,
-            send_sem=ssem.at[p, kind, i],
-            recv_sem=rsem.at[p, got, i],
+            send_sem=ssem.at[p, kind],
+            recv_sem=recv,
             device_id=where,
             device_id_type=MESH,
         )
 
+    def whole(p, block, act):
+        def of(n):
+            act(pl.ds(pl.multiple_of(block * ROWS, CH), n))
+
+        pl.when(block != 3)(lambda: of(ROWS))
+        pl.when(block == 3)(lambda: of(LAST * CH))
+
     sibling = at(y, x, 1 - c, z)
     sends = (
         (FAR, source, RP, at(0, xfar, c, z)),
+        (FAR2, straight, RX, (4, z)),
         (F1, has_f1, RP, at(y1, x, c, z)),
         (F2, has_f2, RP, at(y2, x, c, z)),
-        (FAR2, straight, RX, (4, z)),
-        (EX, has_ex, ex_got, ex_to),
-        (SIBP, has_sib, RSP, sibling),
     )
-
+    ex_to = at(y, other, c, z)
+    plain_ex = (has_ex == 1) & (r != 2) & (straight == 0)
     onward = (
-        (G1, third * has_f1, RX, at(y1, x, c, z)),
-        (G2, third * has_f2, RX, at(y2, x, c, z)),
-        (SIBS, has_sib, RSS, sibling),
+        (G1, third * has_f1, at(y1, x, c, z)),
+        (G2, third * has_f2, at(y2, x, c, z)),
     )
 
     def first(p):
         def issue(i, own):
+            rows = rows_of(mine, i)
+            src = m_ref.at[rows_of(0, i), pl.ds(*PARTS[p])] if own else None
             for kind, has, got, where in sends:
 
                 @pl.when(has == 1)
                 def _(kind=kind, got=got, where=where):
-                    copy(p, mine, i, kind, got, where, own).start()
+                    moved(p, rows, kind, rsem.at[p, got, i], where, src).start()
+
+            @pl.when(plain_ex)
+            def _():
+                moved(p, rows, EX, rsem.at[p, RX, i], ex_to, src).start()
+
+            @pl.when(r == 2)
+            def _():
+                moved(p, rows, EX, ysem.at[p, SS], (1, z), src).start()
+
+            @pl.when(has_sib == 1)
+            def _():
+                moved(p, rows, SIBP, ysem.at[p, SP], sibling, src).start()
 
         def body(i, carry):
             @pl.when(source == 1)
@@ -234,70 +249,67 @@
 
             @pl.when(source == 0)
             def _():
-                copy(p, mine, i, F1, RP, sibling).wait_recv()
+                moved(p, rows_of(mine, i), F1, rsem.at[p, RP, i], sibling).wait_recv()
                 issue(i, False)
 
             return carry
 
         lax.fori_loop(0, n_mine, body, 0)
+
+        @pl.when(straight == 1)
+        def _():
+            def exchange(i, carry):
+                src = m_ref.at[rows_of(0, i), pl.ds(*PARTS[p])]
+                moved(p, rows_of(mine, i), EX, rsem.at[p, RX, i], ex_to, src).start()
+                return carry
+
+            lax.fori_loop(0, NCH, exchange, 0)
 
     def second(p):
         def body(i, carry):
-            copy(p, theirs, i, EX, RX, sibling).wait_recv()
-
-            for kind, has, got, where in onward:
-
-                @pl.when(has == 1)
-                def _(kind=kind, got=got, where=where):
-                    copy(p, theirs, i, kind, got, where).start()
-
-            return carry
-
-        def got_p(i, carry):
-            copy(p, sib_p, i, SIBP, RSP, sibling).wait_recv()
-            return carry
-
-        def got_s(i, carry):
-            copy(p, sib_s, i, SIBS, RSS, sibling).wait_recv()
+            rows = rows_of(theirs, i)
+            moved(p, rows, SIBS, rsem.at[p, RX, i], sibling).wait_recv()
+
+            @pl.when(third == 1)
+            def _():
+                for kind, has, where in onward:
+
+                    @pl.when(has == 1)
+                    def _(kind=kind, where=where):
+                        moved(p, rows, kind, rsem.at[p, RX, i], where).start()
+
+            @pl.when(has_sib == 1)
+            def _():
+                moved(p, rows, SIBS, ysem.at[p, SS], sibling).start()
+
             return carry
 
         @pl.when(busy == 1)
         def _():
             lax.fori_loop(0, n_theirs, body, 0)
-            lax.fori_loop(0, n_sib_p, got_p, 0)
-            lax.fori_loop(0, n_sib_s, got_s, 0)
+            whole(p, sib_p, lambda rows: moved(p, rows, SIBP, ysem.at[p, SP], sibling).wait_recv())
+            whole(p, sib_s, lambda rows: moved(p, rows, SIBS, ysem.at[p, SS], sibling).wait_recv())
 
     def sent(p):
-        def body_p(i, carry):
-            for kind, has, got, where in sends:
-
-                @pl.when(has == 1)
-                def _(kind=kind, got=got, where=where):
-                    copy(p, mine, i, kind, got, where).wait_send()
-
-            return carry
-
-        def body_s(i, carry):
-            for kind, has, got, where in onward:
-
-                @pl.when(has == 1)
-                def _(kind=kind, got=got, where=where):
-                    copy(p, theirs, i, kind, got, where).wait_send()
-
-            return carry
-
-        lax.fori_loop(0, n_mine, body_p, 0)
-
-        @pl.when(busy == 1)
-        def _():
-            lax.fori_loop(0, n_theirs, body_s, 0)
+        def done(kind, block):
+            whole(p, block, lambda rows: moved(p, rows, kind, rsem.at[p, RP, 0], sibling).wait_send())
+
+        for kind, has, _, _ in sends:
+            pl.when(has == 1)(lambda kind=kind: done(kind, mine))
+
+        for kind, has, _ in onward:
+            pl.when(has == 1)(lambda kind=kind: done(kind, theirs))
+
+        pl.when(has_ex == 1)(lambda: done(EX, mine))
+        pl.when(has_sib == 1)(lambda: done(SIBP, mine))
+        pl.when((busy == 1) & (has_sib == 1))(lambda: done(SIBS, theirs))
 
     def wcopy(i, kind, where):
         ref = wbuf.at[pl.ds(pl.multiple_of(i * CZ, CZ), CZ)]
         return pltpu.make_async_remote_copy(
             src_ref=ref,
             dst_ref=ref,
-            send_sem=zssem.at[kind, i],
+            send_sem=zssem.at[kind],
             recv_sem=zrsem.at[i],
             device_id=where,
             device_id_type=MESH,
@@ -325,14 +337,19 @@
 
         lax.fori_loop(0, NCZ, along, 0)
 
-    def along_sent(i, carry):
+    def passed():
         for kind, has, where in down:
 
             @pl.when(has == 1)
             def _(kind=kind, where=where):
-                wcopy(i, kind, where).wait_send()
-
-        return carry
+                pltpu.make_async_remote_copy(
+                    src_ref=wbuf,
+                    dst_ref=wbuf,
+                    send_sem=zssem.at[kind],
+                    recv_sem=zrsem.at[0],
+                    device_id=where,
+                    device_id_type=MESH,
+                ).wait_send()
 
     def give(k):
         cols = pl.ds(k * B, B)
@@ -397,6 +414,8 @@
                 uhigh[:, start : start + B], ulow[:, start : start + B] = split(ubuf[:, start : start + B])
 
         pl.when(has_z1 == 0)(prepare)
+        sent(0)
+        sent(1)
         pl.when(jnp.logical_not(pass_first))(pass_on)
         pl.when(has_z1 == 1)(prepare)
         wh, wl = split(wbuf[...])
@@ -415,9 +434,12 @@
         for k in range(COLS // B):
             give(k).start()
 
-    sent(0)
-    sent(1)
-    lax.fori_loop(0, NCZ, along_sent, 0)
+    @pl.when((z == 0) | (idle == 1))
+    def _():
+        sent(0)
+        sent(1)
+
+    passed()
     for k in range(COLS // B):
         give(k).wait()
 
@@ -435,9 +457,10 @@
             pltpu.VMEM((ROWS, B), jnp.float32),
             pltpu.VMEM((2 * B, COLS), jnp.bfloat16),
             pltpu.VMEM((2 * B, COLS), jnp.bfloat16),
-            pltpu.SemaphoreType.DMA((2, 9, NCH)),
-            pltpu.SemaphoreType.DMA((2, 4, NCH)),
-            pltpu.SemaphoreType.DMA((2, NCZ)),
+            pltpu.SemaphoreType.DMA((2, 9)),
+            pltpu.SemaphoreType.DMA((2, 2, NCH)),
+            pltpu.SemaphoreType.DMA((2, 2)),
+            pltpu.SemaphoreType.DMA((2,)),
             pltpu.SemaphoreType.DMA((NCZ,)),
             pltpu.SemaphoreType.DMA((2,)),
             pltpu.SemaphoreType.DMA((COLS // B,)),

time: 44.8 us -> 40.5 us (0.904)
  the two profiles are of different devices: /device:TPU:292 before, /device:TPU:550 now
where the time goes in v3:
time: 40.5 us; the launch traced here: 40.4 us
  Pallas kernels  39.6 us (98%)
  local copies, waits for them, and re-layouts  0.76 us (2%)
    pallas_call x1, Pallas kernels, on_device(): pl.pallas_call(kernel, out_shape=jax.ShapeDtypeStruct((ROWS, COLS), jnp.f...  39.6 us

profile of v3, /device:TPU:550, one launch (start us, length us, event | category | flops | bytes accessed | tf_op | source)
XLA Modules:
  0.0 40.4 jit_solution(13448643563649479726)
XLA Ops:
  0.0 39.6 %panel_steps.1 = f32[144,768]{1,0:T(8,128)S(1)} custom-call(f32[144,768]{1,0:T(8,128)} %m_ref.1), custom_call_target="tpu_custom_call" | custom-call | tf_op jit(solution)/shard_map/panel_steps/pallas_call | solution.py:448
  39.6 0.8 %copy.3 = f32[144,768]{1,0:T(8,128)} copy(f32[144,768]{1,0:T(8,128)S(1)} %panel_steps.1) | data formatting | bytes 884736

commit v4 on v3

--- a/solution.py
+++ b/solution.py
@@ -10,9 +10,9 @@
 NX, NY, NZ = 4, 8, 12
 CH = 16
 NCH = ROWS // CH
-CZ = 8
+CZ = 16
 NCZ = ROWS // CZ
-LAST = (2 * B - 3 * ROWS) // CH
+LAST = -(-(2 * B - 3 * ROWS) // CH)
 PARTS = ((0, 2 * B), (2 * B, COLS - 2 * B))
 MESH = pl.DeviceIdType.MESH
 VMEM = 54500 << 10
@@ -31,6 +31,7 @@
     6: (5, 7),
     7: (8, None),
 }
+HALF, HALF_FROM, HALF_PARENT = 8, 9, 7
 EARLY = (5, 6)
 PASS_FIRST = 9
 
@@ -68,15 +69,19 @@
     return dot(ah, bh) + (dot(ah, bl) + dot(al, bh))
 
 
-def inverse_of(block):
+def factors_of(block):
     i = lax.broadcasted_iota(jnp.int32, (B, B), 0)
     j = lax.broadcasted_iota(jnp.int32, (B, B), 1)
     diag = jnp.where(i == j, block, 0.0)
     two = jnp.where(i == j, 2.0, 0.0)
     across = 1.0 / jnp.sum(diag, axis=0, keepdims=True)
     down = 1.0 / jnp.sum(diag, axis=1, keepdims=True)
-    first = down * (two - block * across)
-    return mult(first, two - mult(block, first))
+    return split(down * (two - block * across)), two
+
+
+def times(a, pair):
+    ah, al = split(a)
+    return dot(ah, pair[0]) + (dot(ah, pair[1]) + dot(al, pair[0]))
 
 
 def kernel(m_ref, o_ref, tile, ubuf, wbuf, low0, uhigh, ulow, ssem, rsem, ysem, zssem, zrsem, lsem, osem, zready):
@@ -106,6 +111,7 @@
     early2, _ = lookup(z2, {k: 0 for k in EARLY})
     early1, early2 = has_z1 * early1, has_z2 * early2
     late1, late2 = has_z1 - early1, has_z2 - early2
+    gives_half = jnp.where(z == HALF_FROM, busy, 0)
     xfar = NX - 1 - x
     straight = jnp.where((z == 0) & (r == 0), 1, 0)
     third = jnp.where((z == 0) & (c == 0) & (x == 2), 1, 0)
@@ -126,7 +132,7 @@
 
     def own(n):
         return pltpu.make_async_copy(
-            m_ref.at[pl.ds(0, n)], ubuf.at[pl.ds(pl.multiple_of(mine * ROWS, CH), n)], lsem.at[1]
+            m_ref.at[pl.ds(0, n)], ubuf.at[pl.ds(pl.multiple_of(mine * ROWS, 8), n)], lsem.at[1]
         )
 
     @pl.when(full)
@@ -154,6 +160,10 @@
     def _():
         hello((r, zup))
 
+    @pl.when((z == HALF) & (busy == 1))
+    def _():
+        hello((r, HALF_FROM))
+
     @pl.when(late1 == 1)
     def _():
         hello((r, z1))
@@ -179,14 +189,14 @@
         hello((2, z))
 
     greeted = jnp.where((has_zup == 1) & (early == 0), 1, 0)
-    pl.semaphore_wait(bar, has_ex + straight + has_sib + has_f1 + has_f2 + source + early1 + early2 + greeted)
+    pl.semaphore_wait(bar, has_ex + straight + has_sib + has_f1 + has_f2 + source + early1 + early2 + gives_half + greeted)
 
     @pl.when(greeted == 1)
     def _():
         pl.semaphore_signal(zready, inc=1, device_id=(r, zup), device_id_type=MESH)
 
     def rows_of(block, i):
-        return pl.ds(pl.multiple_of(block * ROWS + i * CH, CH), CH)
+        return pl.ds(pl.multiple_of(block * ROWS + i * CH, 8), CH)
 
     def moved(p, rows, kind, recv, where, src=None):
         ref = ubuf.at[rows, pl.ds(*PARTS[p])]
@@ -201,7 +211,7 @@
 
     def whole(p, block, act):
         def of(n):
-            act(pl.ds(pl.multiple_of(block * ROWS, CH), n))
+            act(pl.ds(pl.multiple_of(block * ROWS, 8), n))
 
         pl.when(block != 3)(lambda: of(ROWS))
         pl.when(block == 3)(lambda: of(LAST * CH))
@@ -304,52 +314,68 @@
         pl.when(has_sib == 1)(lambda: done(SIBP, mine))
         pl.when((busy == 1) & (has_sib == 1))(lambda: done(SIBS, theirs))
 
-    def wcopy(i, kind, where):
-        ref = wbuf.at[pl.ds(pl.multiple_of(i * CZ, CZ), CZ)]
+    def wcopy(h, i, kind, where):
+        ref = wbuf.at[h, pl.ds(pl.multiple_of(i * CZ, CZ), CZ)]
         return pltpu.make_async_remote_copy(
             src_ref=ref,
             dst_ref=ref,
             send_sem=zssem.at[kind],
-            recv_sem=zrsem.at[i],
+            recv_sem=zrsem.at[h, i],
             device_id=where,
             device_id_type=MESH,
         )
 
     down = ((0, has_z1, (r, z1)), (1, has_z2, (r, z2)))
 
-    def along(i, carry):
-        @pl.when(has_zup == 1)
-        def _():
-            wcopy(i, 0, (r, z1)).wait_recv()
-
-        for kind, has, where in down:
-
-            @pl.when(has == 1)
-            def _(kind=kind, where=where):
-                wcopy(i, kind, where).start()
-
-        return carry
-
-    def pass_on():
+    def along(h):
+        def body(i, carry):
+            @pl.when(has_zup == 1)
+            def _():
+                wcopy(h, i, 0, (r, z1)).wait_recv()
+
+            for kind, has, where in down:
+
+                @pl.when(has == 1 if h == 1 else (has == 1) & (z != HALF_PARENT))
+                def _(kind=kind, where=where):
+                    wcopy(h, i, kind, where).start()
+
+            return carry
+
+        lax.fori_loop(0, NCZ, body, 0)
+
+    def children():
         @pl.when(late1 + late2 > 0)
         def _():
             pl.semaphore_wait(zready, late1 + late2)
 
-        lax.fori_loop(0, NCZ, along, 0)
+    def pass_on():
+        children()
+        along(1)
+        along(0)
+
+        @pl.when(gives_half == 1)
+        def _():
+            def body(i, carry):
+                wcopy(0, i, 2, (r, HALF)).start()
+                return carry
+
+            lax.fori_loop(0, NCZ, body, 0)
 
     def passed():
-        for kind, has, where in down:
-
-            @pl.when(has == 1)
-            def _(kind=kind, where=where):
-                pltpu.make_async_remote_copy(
-                    src_ref=wbuf,
-                    dst_ref=wbuf,
-                    send_sem=zssem.at[kind],
-                    recv_sem=zrsem.at[0],
-                    device_id=where,
-                    device_id_type=MESH,
-                ).wait_send()
+        def gone(ref, kind):
+            pltpu.make_async_remote_copy(
+                src_ref=ref,
+                dst_ref=ref,
+                send_sem=zssem.at[kind],
+                recv_sem=zrsem.at[0, 0],
+                device_id=(r, z1),
+                device_id_type=MESH,
+            ).wait_send()
+
+        pl.when((has_z1 == 1) & (z == HALF_PARENT))(lambda: gone(wbuf.at[1], 0))
+        pl.when((has_z1 == 1) & (z != HALF_PARENT))(lambda: gone(wbuf, 0))
+        pl.when(has_z2 == 1)(lambda: gone(wbuf, 1))
+        pl.when(gives_half == 1)(lambda: gone(wbuf.at[0], 2))
 
     def give(k):
         cols = pl.ds(k * B, B)
@@ -363,11 +389,12 @@
     pass_first = (z == PASS_FIRST) & (busy == 1)
     first(0)
 
+    pl.when(pass_first)(pass_on)
+
     @pl.when(ahead)
     def _():
         first(1)
 
-    pl.when(pass_first)(pass_on)
     second(0)
     load.wait()
 
@@ -381,25 +408,24 @@
 
     @pl.when((z == 0) & (busy == 1))
     def _():
-        second0 = inverse_of(ubuf[:B, :B])
-        s0 = split(second0)
-
-        def times(a, pair):
-            ah, al = split(a)
-            return dot(ah, pair[0]) + (dot(ah, pair[1]) + dot(al, pair[0]))
-
-        l10 = times(ubuf[B : 2 * B, :B], s0)
-        lower0 = times(tile[:, :B], s0)
+        first0, two = factors_of(ubuf[:B, :B])
+        rest0 = split(two - times(ubuf[:B, :B], first0))
+        l10 = times(times(ubuf[B : 2 * B, :B], first0), rest0)
+        lower0 = times(times(tile[:, :B], first0), rest0)
         u01 = split(ubuf[:B, B : 2 * B])
         block1 = ubuf[B : 2 * B, B : 2 * B] - times(l10, u01)
         panel1 = tile[:, B : 2 * B] - times(lower0, u01)
-        lower1 = mult(panel1, inverse_of(block1))
+        first1, _ = factors_of(block1)
+        rest1 = split(two - times(block1, first1))
+        lower1 = times(times(panel1, first1), rest1)
+        wbuf[1] = jnp.where(below1, lower1, 0.0)
+        children()
+        along(1)
         w0 = lower0 - mult(lower1, l10)
-        wbuf[:, :B] = jnp.where(below1, w0, jnp.where(below0, lower0, 0.0))
-        wbuf[:, B:] = jnp.where(below1, lower1, 0.0)
+        wbuf[0] = jnp.where(below1, w0, jnp.where(below0, lower0, 0.0))
+        along(0)
         low0[...] = lower0
         tile[:, B : 2 * B] = jnp.where(below1, lower1, jnp.where(below0, panel1, tile[:, B : 2 * B]))
-        pass_on()
 
     @pl.when(jnp.logical_not(ahead))
     def _():
@@ -407,26 +433,42 @@
 
     second(1)
 
-    @pl.when((z != 0) & (busy == 1))
-    def _():
-        def prepare():
-            for start in range(0, COLS, B):
-                uhigh[:, start : start + B], ulow[:, start : start + B] = split(ubuf[:, start : start + B])
-
-        pl.when(has_z1 == 0)(prepare)
+    def prepare():
+        for start in range(0, COLS, B):
+            uhigh[:, start : start + B], ulow[:, start : start + B] = split(ubuf[: 2 * B, start : start + B])
+
+    def update(h):
+        wh, wl = split(wbuf[h])
+        for k in range(COLS // B):
+            uh, ul = (u[h * B : (h + 1) * B, k * B : (k + 1) * B] for u in (uhigh, ulow))
+            tile[:, k * B : (k + 1) * B] -= dot(wh, uh) + (dot(wh, ul) + dot(wl, uh))
+            if h == 0:
+                give(k).start()
+
+    @pl.when((z != 0) & (busy == 1) & (has_z1 == 1))
+    def _():
         sent(0)
         sent(1)
         pl.when(jnp.logical_not(pass_first))(pass_on)
-        pl.when(has_z1 == 1)(prepare)
-        wh, wl = split(wbuf[...])
-        for k in range(COLS // B):
-            uh, ul = uhigh[:, k * B : (k + 1) * B], ulow[:, k * B : (k + 1) * B]
-            tile[:, k * B : (k + 1) * B] -= dot(wh, uh) + (dot(wh, ul) + dot(wl, uh))
-            give(k).start()
+        prepare()
+        update(1)
+        update(0)
+
+    @pl.when((z != 0) & (busy == 1) & (has_z1 == 0))
+    def _():
+        prepare()
+        sent(0)
+        sent(1)
+        along(1)
+        update(1)
+        along(0)
+        update(0)
 
     @pl.when((z == 0) & (busy == 1))
     def _():
-        tile[:, 2 * B :] -= mult(wbuf[...], ubuf[:, 2 * B :])
+        for h in range(2):
+            tile[:, 2 * B :] -= mult(wbuf[h], ubuf[h * B : (h + 1) * B, 2 * B :])
+
         tile[:, :B] = jnp.where(below0, low0[...], tile[:, :B])
 
     @pl.when((z == 0) | (idle == 1))
@@ -452,16 +494,16 @@
         out_specs=pl.BlockSpec(memory_space=pl.ANY),
         scratch_shapes=[
             pltpu.VMEM((ROWS, COLS), jnp.float32),
-            pltpu.VMEM((2 * B, COLS), jnp.float32),
-            pltpu.VMEM((ROWS, 2 * B), jnp.float32),
+            pltpu.VMEM((3 * ROWS + LAST * CH, COLS), jnp.float32),
+            pltpu.VMEM((2, ROWS, B), jnp.float32),
             pltpu.VMEM((ROWS, B), jnp.float32),
             pltpu.VMEM((2 * B, COLS), jnp.bfloat16),
             pltpu.VMEM((2 * B, COLS), jnp.bfloat16),
             pltpu.SemaphoreType.DMA((2, 9)),
             pltpu.SemaphoreType.DMA((2, 2, NCH)),
             pltpu.SemaphoreType.DMA((2, 2)),
-            pltpu.SemaphoreType.DMA((2,)),
-            pltpu.SemaphoreType.DMA((NCZ,)),
+            pltpu.SemaphoreType.DMA((3,)),
+            pltpu.SemaphoreType.DMA((2, NCZ)),
             pltpu.SemaphoreType.DMA((2,)),
             pltpu.SemaphoreType.DMA((COLS // B,)),
             pltpu.SemaphoreType.REGULAR,

time: 40.5 us -> 38.9 us (0.960)
  the two profiles are of different devices: /device:TPU:550 before, /device:TPU:292 now
where the time goes in v4:
time: 38.9 us; the launch traced here: 38.8 us
  Pallas kernels  38 us (98%)
  local copies, waits for them, and re-layouts  0.76 us (2%)
    pallas_call x1, Pallas kernels, on_device(): pl.pallas_call(kernel, out_shape=jax.ShapeDtypeStruct((ROWS, COLS), jnp.f...  38 us

profile of v4, /device:TPU:292, one launch (start us, length us, event | category | flops | bytes accessed | tf_op | source)
XLA Modules:
  0.0 38.8 jit_solution(15755941513399607271)
XLA Ops:
  0.0 38.0 %panel_steps.1 = f32[144,768]{1,0:T(8,128)S(1)} custom-call(f32[144,768]{1,0:T(8,128)} %m_ref.1), custom_call_target="tpu_custom_call" | custom-call | tf_op jit(solution)/shard_map/panel_steps/pallas_call | solution.py:490
  38.0 0.8 %copy.3 = f32[144,768]{1,0:T(8,128)} copy(f32[144,768]{1,0:T(8,128)S(1)} %panel_steps.1) | data formatting | bytes 884736

commit v5 on v4

--- a/solution.py
+++ b/solution.py
@@ -8,7 +8,7 @@
 B = 256
 ROWS, COLS = 144, 768
 NX, NY, NZ = 4, 8, 12
-CH = 16
+CH = 8
 NCH = ROWS // CH
 CZ = 16
 NCZ = ROWS // CZ
@@ -218,10 +218,10 @@
 
     sibling = at(y, x, 1 - c, z)
     sends = (
+        (F1, has_f1, RP, at(y1, x, c, z)),
+        (F2, has_f2, RP, at(y2, x, c, z)),
         (FAR, source, RP, at(0, xfar, c, z)),
         (FAR2, straight, RX, (4, z)),
-        (F1, has_f1, RP, at(y1, x, c, z)),
-        (F2, has_f2, RP, at(y2, x, c, z)),
     )
     ex_to = at(y, other, c, z)
     plain_ex = (has_ex == 1) & (r != 2) & (straight == 0)
@@ -234,15 +234,19 @@
         def issue(i, own):
             rows = rows_of(mine, i)
             src = m_ref.at[rows_of(0, i), pl.ds(*PARTS[p])] if own else None
-            for kind, has, got, where in sends:
+            for kind, has, got, where in sends if own else sends[:2]:
 
                 @pl.when(has == 1)
                 def _(kind=kind, got=got, where=where):
                     moved(p, rows, kind, rsem.at[p, got, i], where, src).start()
 
-            @pl.when(plain_ex)
+            @pl.when(plain_ex if own else has_ex == 1)
             def _():
                 moved(p, rows, EX, rsem.at[p, RX, i], ex_to, src).start()
+
+            if not own:
+                moved(p, rows, SIBP, ysem.at[p, SP], sibling).start()
+                return
 
             @pl.when(r == 2)
             def _():

time: 38.9 us -> 38.4 us (0.987)
  the two profiles are of different devices: /device:TPU:292 before, /device:TPU:294 now
where the time goes in v5:
time: 38.4 us; the launch traced here: 38.3 us
  Pallas kernels  37.5 us (98%)
  local copies, waits for them, and re-layouts  0.76 us (2%)
    pallas_call x1, Pallas kernels, on_device(): pl.pallas_call(kernel, out_shape=jax.ShapeDtypeStruct((ROWS, COLS), jnp.f...  37.5 us

profile of v5, /device:TPU:294, one launch (start us, length us, event | category | flops | bytes accessed | tf_op | source)
XLA Modules:
  0.0 38.3 jit_solution(5738614980636709091)
XLA Ops:
  0.0 37.5 %panel_steps.1 = f32[144,768]{1,0:T(8,128)S(1)} custom-call(f32[144,768]{1,0:T(8,128)} %m_ref.1), custom_call_target="tpu_custom_call" | custom-call | tf_op jit(solution)/shard_map/panel_steps/pallas_call | solution.py:494
  37.5 0.8 %copy.3 = f32[144,768]{1,0:T(8,128)} copy(f32[144,768]{1,0:T(8,128)S(1)} %panel_steps.1) | data formatting | bytes 884736

commit v6 on v5

--- a/solution.py
+++ b/solution.py
@@ -252,7 +252,7 @@
             def _():
                 moved(p, rows, EX, ysem.at[p, SS], (1, z), src).start()
 
-            @pl.when(has_sib == 1)
+            @pl.when((has_sib == 1) & (straight == 0))
             def _():
                 moved(p, rows, SIBP, ysem.at[p, SP], sibling, src).start()
 
@@ -275,6 +275,7 @@
             def exchange(i, carry):
                 src = m_ref.at[rows_of(0, i), pl.ds(*PARTS[p])]
                 moved(p, rows_of(mine, i), EX, rsem.at[p, RX, i], ex_to, src).start()
+                moved(p, rows_of(mine, i), SIBP, ysem.at[p, SP], sibling, src).start()
                 return carry
 
             lax.fori_loop(0, NCH, exchange, 0)

time: 38.4 us -> 38.4 us (level)
  no operation moved by 1% of the time
where the time goes in v6:
time: 38.4 us; the launch traced here: 38.3 us
  Pallas kernels  37.5 us (98%)
  local copies, waits for them, and re-layouts  0.76 us (2%)
    pallas_call x1, Pallas kernels, on_device(): pl.pallas_call(kernel, out_shape=jax.ShapeDtypeStruct((ROWS, COLS), jnp.f...  37.5 us

profile of v6, /device:TPU:294, one launch (start us, length us, event | category | flops | bytes accessed | tf_op | source)
XLA Modules:
  0.0 38.3 jit_solution(17393775184213264310)
XLA Ops:
  0.0 37.5 %panel_steps.1 = f32[144,768]{1,0:T(8,128)S(1)} custom-call(f32[144,768]{1,0:T(8,128)} %m_ref.1), custom_call_target="tpu_custom_call" | custom-call | tf_op jit(solution)/shard_map/panel_steps/pallas_call | solution.py:495
  37.5 0.8 %copy.3 = f32[144,768]{1,0:T(8,128)} copy(f32[144,768]{1,0:T(8,128)S(1)} %panel_steps.1) | data formatting | bytes 884736
